TPU v7x, 128 devices: a whole 4x4x4 slice. The times are simulated.
128 devices in a mesh: dom: 32 (over x, z, core), grp: 4 (over y).
Axes of the slice: x: 4, y: 4, z: 4, core: 2. Of those that a mesh axis runs over, the one named last changes fastest.
Arguments:
- embed: float32 [32768, 256], P('dom'), may hold values from -6 to 6
- cotangent: float32 [32768, 256], P('dom'), may hold values from -6 to 6
- first_moment: float32 [32768, 256], P('dom'), may hold values from -4 to 4
- second_moment: float32 [32768, 256], P('dom'), may hold values from 0.1 to 4
- degrees: int32 [32768], P('dom'), may hold values from 16 to 128
- tiles: float32 [32, 4, 128, 128, 128], P('dom', 'grp'), may hold values from 0.05 to 1
- tile_rows: int32 [32, 4, 128], P('dom', 'grp'), may hold values from 0 to 7, as said below
- tile_cols: int32 [32, 4, 128], P('dom', 'grp'), may hold values from 0 to 39
- tile_count: int32 [32, 4], P('dom', 'grp'), may hold values from 16 to 128, as said below
- send_list: int32 [32, 32, 1], P('dom'), may hold values from 0 to 7
Outputs:
- final: float32 [32768, 256], P('dom')
- new_embed: float32 [32768, 256], P('dom')
- new_first: float32 [32768, 256], P('dom')
- new_second: float32 [32768, 256], P('dom')
Inputs may be any that keep to these rules, and one draw needn't show every extreme that they name: `tile_rows`: a row block of the partition; in every partition one hub block holds about half of all tile slots, spread over all helpers. `tile_count`: in every partition one helper has all 128 slots live, the others between 16 and 64.
All inputs are finite; a program needn't handle non-finite values.
Results may differ from a plain program's by a relative error of at most 0.0003.
Values sent between devices are 32-bit elements; how exact they have to be, the bound alone decides.
No kernel may reach another device: no remote copies, remote signals or barrier semaphores. Data moves between devices by JAX's collectives and lax.ppermute only.
A program may use at most 192 MiB of HBM per device.

v0:
```python
import jax
import jax.numpy as jnp
from jax import lax
from jax.sharding import PartitionSpec as P

LAYERS = 2
STEP = 10


def body(
    embed,
    cotangent,
    first_moment,
    second_moment,
    degrees,
    tiles,
    tile_rows,
    tile_cols,
    tile_count,
    send_list,
):
    block_size = tiles.shape[-1]
    feature = embed.shape[1]
    local_blocks = embed.shape[0] // block_size
    partitions = lax.axis_size("dom")
    slot_count = send_list.shape[2]
    readable = local_blocks + partitions * slot_count
    scale = (1.0 / jnp.sqrt(degrees.astype(jnp.float32))).reshape(local_blocks, block_size, 1)
    mats = tiles[0, 0]
    rows = tile_rows[0, 0]
    cols = tile_cols[0, 0]
    live = (jnp.arange(mats.shape[0]) < tile_count[0, 0]).astype(jnp.float32)[:, None, None]
    row_table = (rows[:, None] == jnp.arange(local_blocks)[None, :]).astype(jnp.float32)
    col_table = (cols[:, None] == jnp.arange(readable)[None, :]).astype(jnp.float32)
    targets = send_list[0]
    own_table = (targets[:, :, None] == jnp.arange(local_blocks)[None, None, :]).astype(jnp.float32)
    current = embed.reshape(local_blocks, block_size, feature)
    total_layers = current
    for layer_index in range(LAYERS):
        forward_scaled = scale * current
        outgoing = forward_scaled[targets]
        arrived = lax.all_to_all(outgoing, "dom", split_axis=0, concat_axis=0, tiled=True)
        space = jnp.concatenate(
            [forward_scaled, arrived.reshape(partitions * slot_count, block_size, feature)], 0
        )
        forward_prod = (
            jnp.einsum("tij,tjf->tif", mats, space[cols], precision=lax.Precision.HIGHEST) * live
        )
        partial_sum = jnp.einsum(
            "tb,tif->bif", row_table, forward_prod, precision=lax.Precision.HIGHEST
        )
        current = scale * lax.psum(partial_sum, "grp")
        total_layers = total_layers + current
    final = (total_layers / (LAYERS + 1)).reshape(-1, feature)
    share = cotangent.reshape(local_blocks, block_size, feature) / (LAYERS + 1)
    grad = share
    for layer_index in range(LAYERS):
        scaled = scale * grad
        prod = (
            jnp.einsum("tji,tjf->tif", mats, scaled[rows], precision=lax.Precision.HIGHEST) * live
        )
        contrib = jnp.einsum("tc,tif->cif", col_table, prod, precision=lax.Precision.HIGHEST)
        summed = lax.psum(contrib, "grp")
        remote = summed[local_blocks:].reshape(partitions, slot_count, block_size, feature)
        returned = lax.all_to_all(remote, "dom", split_axis=0, concat_axis=0, tiled=True)
        total = summed[:local_blocks] + jnp.einsum(
            "rsb,rsif->bif", own_table, returned, precision=lax.Precision.HIGHEST
        )
        grad = share + scale * total
    grad = grad.reshape(-1, feature)
    new_first = 0.9 * first_moment + 0.1 * grad
    new_second = 0.999 * second_moment + 0.001 * grad * grad
    corrected_first = new_first / (1.0 - 0.9**STEP)
    corrected_second = new_second / (1.0 - 0.999**STEP)
    new_embed = embed - 0.01 * corrected_first / (jnp.sqrt(corrected_second) + 1e-08)
    return (final, new_embed, new_first, new_second)


def solution(mesh):
    in_specs = (
        P("dom", None),
        P("dom", None),
        P("dom", None),
        P("dom", None),
        P("dom"),
        P("dom", "grp", None, None, None),
        P("dom", "grp", None),
        P("dom", "grp", None),
        P("dom", "grp"),
        P("dom", None, None),
    )
    out_specs = (P("dom", None), P("dom", None), P("dom", None), P("dom", None))
    return jax.shard_map(body, mesh=mesh, in_specs=in_specs, out_specs=out_specs, check_vma=False)
```

profile of v0, /device:TPU:32, one launch (start us, length us, event | category | flops | bytes accessed | tf_op | source)
XLA Modules:
  0.0 798.5 jit_solution(7951557977621942728)
XLA Ops:
  13.8 8.1 %all-to-all-start = ((f32[32,1,128,256]{3,2,1,0:T(8,128)}), f32[32,1,128,256]{3,2,1,0:T(8,128)}, u32[]{:S(2)}, u32[]{:S(2)}) async-start(f32[32,1,128,256]{3,2,1,0:T(8,128)} %bitcast.102), calls=%async_computation | async-start | bytes 8388608 | tf_op jit(solution)/shard_map/all_to_all | solution.py:42
  22.8 7.4 gather_fusion.4
  30.2 36.3 %multiply_bitcast_fusion.1 = f32[128,128,256]{1,2,0:T(8,128)} fusion(f32[128,128,256]{2,1,0:T(8,128)} %gather_fusion.4, f32[1,1,128,128,128]{4,3,2,1,0:T(8,128)} %param.15, f32[128]{0:T(128)S(1)} %compare_convert_fusion), kind=kOutput, calls=%fused_computation.7 | convolution fusion | flops 6446645248 | bytes 41943552 | tf_op jit(solution)/shard_map/tji,tjf->tif/dot_general | solution.py:60
  66.5 17.7 %copy.41 = f32[128,128,256]{2,0,1:T(8,128)} copy(f32[128,128,256]{1,2,0:T(8,128)} %multiply_bitcast_fusion.1) | data formatting | bytes 33554432 | tf_op jit(solution)/shard_map/mul | solution.py:60
  84.2 11.3 %fusion.36 = f32[40,128,256]{2,0,1:T(8,128)} fusion(f32[128,128,256]{2,0,1:T(8,128)} %copy.41, s32[128]{0:T(128)S(1)} %bitcast.112), kind=kOutput, calls=%fused_computation.44 | convolution fusion | flops 2013271040 | bytes 22020608 | tf_op jit(solution)/shard_map/tc,tif->cif/dot_general | solution.py:62
  100.7 12.6 %gather_fusion.1 = f32[128,128,256]{2,1,0:T(8,128)} fusion(f32[40,128,256]{2,1,0:T(8,128)} %pad_maximum_fusion, s32[1024]{0:T(1024)S(1)} %pad_clamp_fusion.1), kind=kCustom, calls=%fused_computation.1 | custom fusion | bytes 33554944 | tf_op jit(solution)/shard_map/gather | solution.py:47
  113.2 36.3 %multiply_bitcast_fusion.3 = f32[128,128,256]{1,2,0:T(8,128)} fusion(f32[128,128,256]{2,1,0:T(8,128)} %gather_fusion.1, f32[1,1,128,128,128]{4,3,2,1,0:T(8,128)} %param.15, f32[128]{0:T(128)S(1)} %compare_convert_fusion), kind=kOutput, calls=%fused_computation.9 | convolution fusion | flops 6446645248 | bytes 41943552 | tf_op jit(solution)/shard_map/tij,tjf->tif/dot_general | solution.py:47
  149.5 17.7 %copy.31 = f32[128,128,256]{2,0,1:T(8,128)} copy(f32[128,128,256]{1,2,0:T(8,128)} %multiply_bitcast_fusion.3) | data formatting | bytes 33554432 | tf_op jit(solution)/shard_map/mul | solution.py:47
  167.1 10.2 %fusion.43 = f32[8,128,256]{2,0,1:T(8,128)} fusion(f32[128,128,256]{2,0,1:T(8,128)} %copy.31, s32[128]{0:T(128)S(1)} %bitcast.110), kind=kOutput, calls=%fused_computation.55 | convolution fusion | flops 402654208 | bytes 17826304 | tf_op jit(solution)/shard_map/tb,tif->bif/dot_general | solution.py:49
  177.3 128.6 %all-reduce.7.cloned.1.call-done = (f32[8,128,256]{2,0,1:T(8,128)}, f32[40,128,256]{2,0,1:T(8,128)}) async-done(((f32[8,128,256]{2,0,1:T(8,128)}, f32[40,128,256]{2,0,1:T(8,128)}), (f32[8,128,256]{2,0,1:T(8,128)}, f32[40,128,256]{2,0,1:T(8,128)})) %all-reduce.7.cloned.1.call-update) | async-done | bytes 6291472 | tf_op jit(solution)/shard_map/psum | solution.py:52
  310.6 7.5 all-to-all-start.1
  325.2 47.5 %all-to-all-done.1 = f32[32,1,128,256]{3,2,1,0:T(8,128)} async-done(((f32[32,1,128,256]{3,2,1,0:T(8,128)}), f32[32,1,128,256]{3,2,1,0:T(8,128)}, u32[]{:S(2)}, u32[]{:S(2)}) %all-to-all-start.1) | async-done | bytes 4194336 | tf_op jit(solution)/shard_map/all_to_all | solution.py:42
  382.8 49.3 %all-to-all-done.2 = f32[32,1,128,256]{3,2,1,0:T(8,128)} async-done(((f32[32,1,128,256]{3,2,1,0:T(8,128)}), f32[32,1,128,256]{3,2,1,0:T(8,128)}, u32[]{:S(2)}, u32[]{:S(2)}) %all-to-all-start.2) | async-done | bytes 4194336 | tf_op jit(solution)/shard_map/all_to_all | solution.py:65
  439.1 12.5 %gather_fusion.3 = f32[128,128,256]{2,1,0:T(8,128)} fusion(f32[40,128,256]{2,1,0:T(8,128)} %pad_maximum_fusion.1, s32[1024]{0:T(1024)S(1)} %pad_clamp_fusion.1), kind=kCustom, calls=%fused_computation.3 | custom fusion | bytes 33554944 | tf_op jit(solution)/shard_map/gather | solution.py:47
  451.6 36.3 %multiply_bitcast_fusion.2 = f32[128,128,256]{1,2,0:T(8,128)} fusion(f32[128,128,256]{2,1,0:T(8,128)} %gather_fusion.3, f32[1,1,128,128,128]{4,3,2,1,0:T(8,128)} %param.15, f32[128]{0:T(128)S(1)} %compare_convert_fusion), kind=kOutput, calls=%fused_computation.8 | convolution fusion | flops 6446645248 | bytes 41943552 | tf_op jit(solution)/shard_map/tij,tjf->tif/dot_general | solution.py:47
  487.9 17.7 %copy.37 = f32[128,128,256]{2,0,1:T(8,128)} copy(f32[128,128,256]{1,2,0:T(8,128)} %multiply_bitcast_fusion.2) | data formatting | bytes 33554432 | tf_op jit(solution)/shard_map/mul | solution.py:47
  505.5 10.0 %fusion.41 = f32[8,128,256]{2,0,1:T(8,128)} fusion(f32[128,128,256]{2,0,1:T(8,128)} %copy.37, s32[128]{0:T(128)S(1)} %bitcast.111), kind=kOutput, calls=%fused_computation.54 | convolution fusion | flops 402654208 | bytes 17826304 | tf_op jit(solution)/shard_map/tb,tif->bif/dot_general | solution.py:49
  515.5 7.4 gather_fusion.5
  522.9 36.1 %multiply_bitcast_fusion = f32[128,128,256]{1,2,0:T(8,128)} fusion(f32[128,128,256]{2,1,0:T(8,128)} %gather_fusion.5, f32[1,1,128,128,128]{4,3,2,1,0:T(8,128)} %param.15, f32[128]{0:T(128)S(1)} %compare_convert_fusion), kind=kOutput, calls=%fused_computation.6 | convolution fusion | flops 6446645248 | bytes 41943552 | tf_op jit(solution)/shard_map/tji,tjf->tif/dot_general | solution.py:60
  559.0 17.6 %copy.46 = f32[128,128,256]{2,0,1:T(8,128)} copy(f32[128,128,256]{1,2,0:T(8,128)} %multiply_bitcast_fusion) | data formatting | bytes 33554432 | tf_op jit(solution)/shard_map/mul | solution.py:60
  576.7 11.6 %fusion.34 = f32[40,128,256]{2,0,1:T(8,128)} fusion(f32[128,128,256]{2,0,1:T(8,128)} %copy.46, s32[128]{0:T(128)S(1)} %bitcast.113), kind=kOutput, calls=%fused_computation.43 | convolution fusion | flops 2013271040 | bytes 22020608 | tf_op jit(solution)/shard_map/tc,tif->cif/dot_general | solution.py:62
  588.3 124.5 %all-reduce.5.cloned.1.call-done = (f32[8,128,256]{2,0,1:T(8,128)}, f32[40,128,256]{2,0,1:T(8,128)}) async-done(((f32[8,128,256]{2,0,1:T(8,128)}, f32[40,128,256]{2,0,1:T(8,128)}), (f32[8,128,256]{2,0,1:T(8,128)}, f32[40,128,256]{2,0,1:T(8,128)})) %all-reduce.5.cloned.1.call-update) | async-done | bytes 6291472 | tf_op jit(solution)/shard_map/psum | solution.py:52
  719.8 8.0 %all-to-all-start.3 = ((f32[32,1,128,256]{3,2,1,0:T(8,128)}), f32[32,1,128,256]{3,2,1,0:T(8,128)}, u32[]{:S(2)}, u32[]{:S(2)}) async-start(f32[32,1,128,256]{3,2,1,0:T(8,128)} %copy.47), calls=%async_computation.3 | async-start | bytes 8388608 | tf_op jit(solution)/shard_map/all_to_all | solution.py:65
  731.1 50.8 %all-to-all-done.3 = f32[32,1,128,256]{3,2,1,0:T(8,128)} async-done(((f32[32,1,128,256]{3,2,1,0:T(8,128)}), f32[32,1,128,256]{3,2,1,0:T(8,128)}, u32[]{:S(2)}, u32[]{:S(2)}) %all-to-all-start.3) | async-done | bytes 4194336 | tf_op jit(solution)/shard_map/all_to_all | solution.py:65
  (54 shorter events, 60.2 us)
Async XLA Ops:
  10.8 11.7 %copy-start.6 = (s32[1,1,128]{2,1,0:T(1,128)S(1)}, s32[1,1,128]{2,1,0:T(1,128)}, u32[]{:S(2)}) copy-start(s32[1,1,128]{2,1,0:T(1,128)} %param.16) | copy-start | bytes 1540
  10.9 11.7 %copy-start.5 = (s32[1024]{0:T(1024)S(1)}, s32[1024]{0:T(1024)}, u32[]{:S(2)}) copy-start(s32[1024]{0:T(1024)} %param.14) | copy-start | bytes 12292
  10.9 11.8 %copy-start.1 = (f32[1024,256]{1,0:T(8,128)S(1)}, f32[1024,256]{1,0:T(8,128)}, u32[]{:S(2)}) copy-start(f32[1024,256]{1,0:T(8,128)} %param.11) | copy-start | bytes 3145732
  13.8 81.7 %all-to-all-start = ((f32[32,1,128,256]{3,2,1,0:T(8,128)}), f32[32,1,128,256]{3,2,1,0:T(8,128)}, u32[]{:S(2)}, u32[]{:S(2)}) async-start(f32[32,1,128,256]{3,2,1,0:T(8,128)} %bitcast.102), calls=%async_computation | async-start | bytes 8388608 | tf_op jit(solution)/shard_map/all_to_all | solution.py:42
  21.9 284.1 %all-reduce.7.cloned.1.call-start = ((), (), s32[]{:S(2)}) async-start(), calls=%async_computation.5 | async-start | bytes 12582912 | tf_op jit(solution)/shard_map/psum | solution.py:52
  66.5 17.7 %copy-start.7 = (s32[1,1,128]{2,1,0:T(1,128)S(1)}, s32[1,1,128]{2,1,0:T(1,128)}, u32[]{:S(2)}) copy-start(s32[1,1,128]{2,1,0:T(1,128)} %param.17) | copy-start | bytes 1540
  310.6 62.1 %all-to-all-start.1 = ((f32[32,1,128,256]{3,2,1,0:T(8,128)}), f32[32,1,128,256]{3,2,1,0:T(8,128)}, u32[]{:S(2)}, u32[]{:S(2)}) async-start(f32[32,1,128,256]{3,2,1,0:T(8,128)} %bitcast.103), calls=%async_computation.1 | async-start | bytes 8388608 | tf_op jit(solution)/shard_map/all_to_all | solution.py:42
  325.2 106.9 %copy-start.8 = (s32[1,32,1]{1,2,0:T(1,128)S(1)}, s32[1,32,1]{1,2,0:T(1,128)}, u32[]{:S(2)}) copy-start(s32[1,32,1]{1,2,0:T(1,128)} %param.19) | copy-start | bytes 388
  372.7 59.4 %all-to-all-start.2 = ((f32[32,1,128,256]{3,2,1,0:T(8,128)}), f32[32,1,128,256]{3,2,1,0:T(8,128)}, u32[]{:S(2)}, u32[]{:S(2)}) async-start(f32[32,1,128,256]{3,2,1,0:T(8,128)} %copy.42), calls=%async_computation.2 | async-start | bytes 8388608 | tf_op jit(solution)/shard_map/all_to_all | solution.py:65
  377.6 335.2 %all-reduce.5.cloned.1.call-start = ((), (), s32[]{:S(2)}) async-start(), calls=%async_computation.4 | async-start | bytes 12582912 | tf_op jit(solution)/shard_map/psum | solution.py:52
  715.3 12.6 %copy-start = (f32[1024,256]{1,0:T(8,128)S(1)}, f32[1024,256]{1,0:T(8,128)}, u32[]{:S(2)}) copy-start(f32[1024,256]{1,0:T(8,128)} %param.10) | copy-start | bytes 3145732
  715.3 12.6 %copy-start.2 = (f32[8,128,256]{2,0,1:T(8,128)S(1)}, f32[8,128,256]{2,0,1:T(8,128)}, u32[]{:S(2)}) copy-start(f32[8,128,256]{2,0,1:T(8,128)} %get-tuple-element.6) | copy-start | bytes 3145732
  719.8 62.1 %all-to-all-start.3 = ((f32[32,1,128,256]{3,2,1,0:T(8,128)}), f32[32,1,128,256]{3,2,1,0:T(8,128)}, u32[]{:S(2)}, u32[]{:S(2)}) async-start(f32[32,1,128,256]{3,2,1,0:T(8,128)} %copy.47), calls=%async_computation.3 | async-start | bytes 8388608 | tf_op jit(solution)/shard_map/all_to_all | solution.py:65
  781.9 7.1 copy-start.3
  781.9 7.1 copy-start.4
Sparse Core Ops, SparseCore 0:
  177.5 128.4 all-reduce.6
  588.4 124.3 all-reduce.4
where the time goes:
time: 803 us; the launch traced here: 798 us
  waiting for transfers between devices  401 us (50%)
  matrix products  201 us (25%)
  local copies, waits for them, and re-layouts  133 us (17%)
  starting transfers between devices  28.5 us (4%)
  other arithmetic  19.2 us (2%)
  between operations  15.4 us (2%)
    psum x2, waiting for transfers between devices, body(): current = scale * lax.psum(partial_sum, 'grp')  253 us
    all_to_all x2, waiting for transfers between devices, body(): lax.all_to_all(remote, 'dom', split_axis=0, concat_axis=0, tiled=True)  100 us
    dot_general x2, matrix products, body(): jnp.einsum('tij,tjf->tif', mats, space[cols], precision=lax.Precision.HIG...  72.5 us
    dot_general x2, matrix products, body(): jnp.einsum('tji,tjf->tif', mats, scaled[rows], precision=lax.Precision.HI...  72.4 us
    all_to_all x2, waiting for transfers between devices, body(): lax.all_to_all(outgoing, 'dom', split_axis=0, concat_axis=0, tiled=True)  47.5 us
    mul x2, local copies, waits for them, and re-layouts, body(): jnp.einsum('tij,tjf->tif', mats, space[cols], precision=lax.Precision.HIG...  35.3 us
    mul x2, local copies, waits for them, and re-layouts, body(): jnp.einsum('tji,tjf->tif', mats, scaled[rows], precision=lax.Precision.HI...  35.3 us
    gather x2, local copies, waits for them, and re-layouts, body(): space[cols]  25.1 us
  transfers between devices with their start and end apart: 6, of which 5 were waited for; matrix products, arithmetic and copies ran while one was open for 11% of the time, Pallas kernels for 0%

commit v1 on v0

v1 whole, which is shorter than its diff:
```python
import functools

import jax
import jax.numpy as jnp
from jax import lax
from jax.experimental import pallas as pl
from jax.experimental.pallas import tpu as pltpu
from jax.sharding import PartitionSpec as P

LAYERS = 2
STEP = 10
CHUNKS = 8
UNROLL = 8
MIB = 2**20

SMEM = pl.BlockSpec(memory_space=pltpu.SMEM)
VMEM = pl.BlockSpec(memory_space=pltpu.VMEM)
ANY = pl.BlockSpec(memory_space=pl.ANY)


def f32(*shape):
    return jax.ShapeDtypeStruct(shape, jnp.float32)


def params(mib):
    return pltpu.CompilerParams(vmem_limit_bytes=mib * MIB)


def cost(us):
    return pl.CostEstimate(flops=0, bytes_accessed=int(us * 3.6e6), transcendentals=0)


def split(x):
    hi = x.astype(jnp.bfloat16)
    lo = (x - hi.astype(jnp.float32)).astype(jnp.bfloat16)
    return hi, lo


def store_split(xs, c, x):
    hi, lo = split(x)
    xs[c, 0:128] = hi
    xs[c, 128:256] = lo
    xs[c, 256:384] = hi


def product(tile, xs, c):
    hi, lo = split(tile)
    return jnp.dot(
        jnp.concatenate([hi, hi, lo], 1), xs[c], preferred_element_type=jnp.float32
    )


def start_tiles(tiles, buf, sems):
    n = tiles.shape[0] // CHUNKS
    copies = [
        pltpu.make_async_copy(tiles.at[pl.ds(i * n, n)], buf.at[pl.ds(i * n, n)], sems.at[i])
        for i in range(CHUNKS)
    ]
    for c in copies:
        c.start()
    return copies


def place_quarters(rank, pieces, full):
    for k, piece in enumerate(pieces):
        at = lax.rem(rank + 4 - k, 4) * 2
        full[pl.ds(at, 2)] = piece[...]


def take_quarters(rank, full, outs):
    for k, out in enumerate(outs):
        at = lax.rem(rank + k, 4) * 2
        out[...] = full[pl.ds(at, 2)]


def send_blocks(targets, source, outgoing):
    def one(p, _):
        outgoing[p] = source[targets[p]]
        return 0

    lax.fori_loop(0, outgoing.shape[0], one, 0)


def first_kernel(targets, embed, scale, scaled, outgoing):
    scaled[...] = embed[...] * scale[...]
    send_blocks(targets, scaled, outgoing)


def next_kernel(rank, targets, scale, q0, q1, q2, q3, scaled, layer, outgoing):
    place_quarters(rank[0], (q0, q1, q2, q3), scaled)
    s = scale[...]
    cur = scaled[...] * s
    layer[...] = cur
    scaled[...] = cur * s
    send_blocks(targets, scaled, outgoing)


def final_kernel(rank, scale, embed, layer, q0, q1, q2, q3, out):
    place_quarters(rank[0], (q0, q1, q2, q3), out)
    out[...] = (embed[...] + layer[...] + out[...] * scale[...]) / 3.0


def forward_kernel(rank, count, rows, cols, own, arrived, tiles, o0, o1, o2, o3, buf, xs, acc, sems):
    copies = start_tiles(tiles, buf, sems)
    local = own.shape[0]

    def split_own(c, _):
        store_split(xs, c, own[c])
        return 0

    def split_arrived(c, _):
        store_split(xs, local + c, arrived[c])
        return 0

    lax.fori_loop(0, local, split_own, 0)
    lax.fori_loop(0, arrived.shape[0], split_arrived, 0)
    acc[...] = jnp.zeros_like(acc)
    for c in copies:
        c.wait()
    live = count[0]

    def step(i, _):
        prods = [product(buf[i * UNROLL + k], xs, cols[i * UNROLL + k]) for k in range(UNROLL)]
        for k in range(UNROLL):
            t = i * UNROLL + k
            acc[jnp.where(t < live, rows[t], local)] += prods[k]
        return 0

    lax.fori_loop(0, (live + UNROLL - 1) // UNROLL, step, 0)
    take_quarters(rank[0], acc, (o0, o1, o2, o3))


def backward_sums(count, rows, cols, tiles, out_local, out_remote, buf, zs, acc, copies):
    local = out_local.shape[0]
    readable = local + out_remote.shape[0]

    def clear(c, _):
        acc[c] = jnp.zeros(acc.shape[1:], jnp.float32)
        return 0

    lax.fori_loop(0, readable + 1, clear, 0)
    for c in copies:
        c.wait()
    live = count[0]

    def step(i, _):
        prods = [product(buf[i * UNROLL + k].T, zs, rows[i * UNROLL + k]) for k in range(UNROLL)]
        for k in range(UNROLL):
            t = i * UNROLL + k
            acc[jnp.where(t < live, cols[t], readable)] += prods[k]
        return 0

    lax.fori_loop(0, (live + UNROLL - 1) // UNROLL, step, 0)

    def put_local(c, _):
        out_local[c] = acc[c]
        return 0

    def put_remote(c, _):
        out_remote[c] = acc[local + c]
        return 0

    lax.fori_loop(0, local, put_local, 0)
    lax.fori_loop(0, out_remote.shape[0], put_remote, 0)


def backward_first_kernel(count, rows, cols, scale, cot, tiles, out_local, out_remote, buf, zs, acc, sems):
    copies = start_tiles(tiles, buf, sems)

    def prepare(b, _):
        store_split(zs, b, cot[b] / 3.0 * scale[b])
        return 0

    lax.fori_loop(0, cot.shape[0], prepare, 0)
    backward_sums(count, rows, cols, tiles, out_local, out_remote, buf, zs, acc, copies)


def backward_next_kernel(
    rank, count, rows, cols, scale, cot, q0, q1, q2, q3, tiles, out_local, out_remote, buf, zs, acc, sems
):
    copies = start_tiles(tiles, buf, sems)
    place_quarters(rank[0], (q0, q1, q2, q3), acc)

    def prepare(b, _):
        s = scale[b]
        store_split(zs, b, (cot[b] / 3.0 + s * acc[b]) * s)
        return 0

    lax.fori_loop(0, cot.shape[0], prepare, 0)
    backward_sums(count, rows, cols, tiles, out_local, out_remote, buf, zs, acc, copies)


def collect_kernel(rank, targets, local, returned, o0, o1, o2, o3, acc):
    acc[...] = local[...]

    def one(r, _):
        acc[targets[r]] += returned[r]
        return 0

    lax.fori_loop(0, returned.shape[0], one, 0)
    take_quarters(rank[0], acc, (o0, o1, o2, o3))


def adam_kernel(
    rank, scale, cot, embed, first, second, q0, q1, q2, q3, new_embed, new_first, new_second
):
    place_quarters(rank[0], (q0, q1, q2, q3), new_first)

    def one(b, _):
        grad = cot[b] / 3.0 + scale[b] * new_first[b]
        m = 0.9 * first[b] + 0.1 * grad
        v = 0.999 * second[b] + 0.001 * grad * grad
        new_first[b] = m
        new_second[b] = v
        step = m / (1.0 - 0.9**STEP)
        new_embed[b] = embed[b] - 0.01 * step / (jnp.sqrt(v / (1.0 - 0.999**STEP)) + 1e-08)
        return 0

    lax.fori_loop(0, embed.shape[0], one, 0)


def call(kernel, outs, ins, args, us, mib, scratch=()):
    return pl.pallas_call(
        kernel,
        out_shape=outs,
        in_specs=ins,
        out_specs=[VMEM] * len(outs),
        scratch_shapes=scratch,
        compiler_params=params(mib),
        cost_estimate=cost(us),
    )(*args)


def shifted(x, by):
    n = lax.axis_size("grp")
    return lax.ppermute(x, "grp", [(i, (i + by) % n) for i in range(n)])


def sum_and_share(parts):
    own = parts[0] + shifted(parts[1], 1) + shifted(parts[2], 2) + shifted(parts[3], 3)
    return (own, shifted(own, 1), shifted(own, 2), shifted(own, 3))


def exchange(x):
    return lax.all_to_all(x, "dom", split_axis=0, concat_axis=0, tiled=True)


def body(
    embed,
    cotangent,
    first_moment,
    second_moment,
    degrees,
    tiles,
    tile_rows,
    tile_cols,
    tile_count,
    send_list,
):
    block = tiles.shape[-1]
    feature = embed.shape[1]
    local = embed.shape[0] // block
    remote = send_list.shape[1] * send_list.shape[2]
    slots = tiles.shape[2]
    rank = lax.axis_index("grp").astype(jnp.int32).reshape(1)
    scale = (1.0 / jnp.sqrt(degrees.astype(jnp.float32))).reshape(local, block, 1)
    mats = tiles[0, 0]
    rows, cols, count = tile_rows[0, 0], tile_cols[0, 0], tile_count[0]
    targets = send_list.reshape(remote)
    as_blocks = lambda x: x.reshape(local, block, feature)
    emb, cot = as_blocks(embed), as_blocks(cotangent)
    blocks, sent, quarter = f32(local, block, feature), f32(remote, block, feature), f32(2, block, feature)
    quarters = [quarter] * 4
    tile_buf = pltpu.VMEM((slots, block, block), jnp.float32)
    sems = pltpu.SemaphoreType.DMA((CHUNKS,))
    right = lambda n: pltpu.VMEM((n, 3 * block, feature), jnp.bfloat16)
    sums = lambda n: pltpu.VMEM((n, block, feature), jnp.float32)

    def forward(own, arrived):
        return call(
            forward_kernel, quarters, [SMEM] * 4 + [VMEM] * 2 + [ANY],
            (rank, count, rows, cols, own, arrived, mats), 14, 28,
            [tile_buf, right(local + remote), sums(local + 1), sems],
        )

    back_scratch = [tile_buf, right(local), sums(local + remote + 1), sems]
    scaled, outgoing = call(
        first_kernel, [blocks, sent], [SMEM, VMEM, VMEM], (targets, emb, scale), 3, 10
    )
    arrived = exchange(outgoing)
    out_local, out_remote = call(
        backward_first_kernel, [blocks, sent], [SMEM] * 3 + [VMEM] * 2 + [ANY],
        (count, rows, cols, scale, cot, mats), 14, 26, back_scratch,
    )
    returned = exchange(out_remote)
    parts = sum_and_share(forward(scaled, arrived))
    scaled, layer, outgoing = call(
        next_kernel, [blocks, blocks, sent], [SMEM] * 2 + [VMEM] * 5,
        (rank, targets, scale, *parts), 3, 12,
    )
    arrived = exchange(outgoing)
    back = call(
        collect_kernel, quarters, [SMEM] * 2 + [VMEM] * 2,
        (rank, targets, out_local, returned), 3, 10, [sums(local)],
    )
    back = sum_and_share(back)
    out_local, out_remote = call(
        backward_next_kernel, [blocks, sent], [SMEM] * 4 + [VMEM] * 6 + [ANY],
        (rank, count, rows, cols, scale, cot, *back, mats), 14, 26, back_scratch,
    )
    returned = exchange(out_remote)
    parts = sum_and_share(forward(scaled, arrived))
    (final,) = call(
        final_kernel, [blocks], [SMEM] + [VMEM] * 7, (rank, scale, emb, layer, *parts), 2, 10
    )
    back = call(
        collect_kernel, quarters, [SMEM] * 2 + [VMEM] * 2,
        (rank, targets, out_local, returned), 3, 10, [sums(local)],
    )
    back = sum_and_share(back)
    new = call(
        adam_kernel, [blocks] * 3, [SMEM] + [VMEM] * 9,
        (rank, scale, cot, emb, as_blocks(first_moment), as_blocks(second_moment), *back), 4, 14,
    )
    flat = lambda x: x.reshape(local * block, feature)
    return (flat(final), *(flat(x) for x in new))


def solution(mesh):
    in_specs = (
        P("dom", None),
        P("dom", None),
        P("dom", None),
        P("dom", None),
        P("dom"),
        P("dom", "grp", None, None, None),
        P("dom", "grp", None),
        P("dom", "grp", None),
        P("dom", "grp"),
        P("dom", None, None),
    )
    out_specs = (P("dom", None), P("dom", None), P("dom", None), P("dom", None))
    return jax.shard_map(body, mesh=mesh, in_specs=in_specs, out_specs=out_specs, check_vma=False)
```

time: 803 us -> 299 us (0.37)
  waiting for transfers between devices: 401 us -> 158 us
  matrix products: 201 us -> 0 us
  local copies, waits for them, and re-layouts: 133 us -> 29 us
  starting transfers between devices: 28.5 us -> 71.1 us
  Pallas kernels: 0 us -> 36.1 us
  other arithmetic: 19.2 us -> 2.07 us
  between operations: 15.4 us -> 1.58 us
    psum x2 -> x0, waiting for transfers between devices: 253 us -> none  [body(): current = scale * lax.psum(partial_sum, 'grp')]
    dot_general x10 -> x0, matrix products: 201 us -> none  [the longest x2 72.5 us: body(): jnp.einsum('tij,tjf->tif', mats, space[cols], precision=lax.Precision.HIG...]
    ppermute x0 -> x24, waiting for transfers between devices: none -> 72.5 us  [shifted(): return lax.ppermute(x, 'grp', [(i, (i + by) % n) for i in range(n)])]
    mul x8 -> x0, local copies, waits for them, and re-layouts: 71.7 us -> none  [the longest x2 35.3 us: body(): jnp.einsum('tij,tjf->tif', mats, space[cols], precision=lax.Precision.HIG...]
    all_to_all x4, waiting for transfers between devices: 148 us -> 85.6 us  [exchange(): return lax.all_to_all(x, 'dom', split_axis=0, concat_axis=0, tiled=True)]
    ppermute x0 -> x24, starting transfers between devices: none -> 47.1 us  [shifted(): return lax.ppermute(x, 'grp', [(i, (i + by) % n) for i in range(n)])]
    gather x6 -> x0, local copies, waits for them, and re-layouts: 45.6 us -> none  [the longest x2 25.1 us: body(): space[cols]]
    pallas_call x0 -> x10, Pallas kernels: none -> 36.1 us  [call(): pl.pallas_call(kernel, out_shape=outs, in_specs=ins, out_specs=[VMEM] * l...]
  transfers between devices with their start and end apart: 6 -> 28, of which waited for: 5 -> 16; matrix products, arithmetic and copies ran while one was open for 11% -> 0% of each run, Pallas kernels for 0% -> 11%
where the time goes in v1:
time: 299 us; the launch traced here: 298 us
  waiting for transfers between devices  158 us (53%)
  starting transfers between devices  71.1 us (24%)
  Pallas kernels  36.1 us (12%)
  local copies, waits for them, and re-layouts  29 us (10%)
    all_to_all x4, waiting for transfers between devices, exchange(): return lax.all_to_all(x, 'dom', split_axis=0, concat_axis=0, tiled=True)  85.6 us
    ppermute x24, waiting for transfers between devices, shifted(): return lax.ppermute(x, 'grp', [(i, (i + by) % n) for i in range(n)])  72.5 us
    ppermute x24, starting transfers between devices, shifted(): return lax.ppermute(x, 'grp', [(i, (i + by) % n) for i in range(n)])  47.1 us
    pallas_call x10, Pallas kernels, call(): pl.pallas_call(kernel, out_shape=outs, in_specs=ins, out_specs=[VMEM] * l...  36.1 us
    unnamed x46, local copies, waits for them, and re-layouts  28.8 us
    all_to_all x4, starting transfers between devices, exchange(): return lax.all_to_all(x, 'dom', split_axis=0, concat_axis=0, tiled=True)  24 us
  transfers between devices with their start and end apart: 28, of which 16 were waited for; matrix products, arithmetic and copies ran while one was open for 0% of the time, Pallas kernels for 11%

profile of v1, /device:TPU:32, one launch (start us, length us, event | category | flops | bytes accessed | tf_op | source)
XLA Modules:
  0.0 298.0 jit_solution(7736588596117422004)
XLA Ops:
  6.6 8.2 %all-to-all-start = ((f32[32,128,256]{2,1,0:T(8,128)}), f32[32,128,256]{2,1,0:T(8,128)}, u32[]{:S(2)}, u32[]{:S(2)}) async-start(f32[32,128,256]{2,1,0:T(8,128)} %copy-done.10), calls=%async_computation | async-start | bytes 8388608 | tf_op jit(solution)/shard_map/all_to_all | solution.py:245
  18.9 5.3 %shard_map.134 = (f32[8,128,256]{2,1,0:T(8,128)S(1)}, f32[32,128,256]{2,1,0:T(8,128)S(1)}) custom-call(s32[1]{0:T(128)} %bitcast.18.count, s32[128]{0:T(128)S(1)} %bitcast.36, s32[128]{0:T(128)S(1)} %bitcast.40, f32[8,128,1]{2,1,0:T(8,128)S(1)} %copy.16.scale, f32[8,128,256]{2,1,0:T(8,128)S(1)} %bitcast.27, f32[128,128,128]{2,1,0:T(8,128)S(1)} %bitcast.20), custom_call_target="tpu_custom_call" | custom-call | bytes 50400000 | tf_op jit(solution)/shard_map/pallas_call | solution.py:223
  27.2 42.2 %all-to-all-done.arrived = f32[32,128,256]{2,1,0:T(8,128)} async-done(((f32[32,128,256]{2,1,0:T(8,128)}), f32[32,128,256]{2,1,0:T(8,128)}, u32[]{:S(2)}, u32[]{:S(2)}) %all-to-all-start) | async-done | bytes 4194336 | tf_op jit(solution)/shard_map/all_to_all | solution.py:245
  69.4 4.8 %all-to-all-start.2 = ((f32[32,128,256]{2,1,0:T(8,128)}), f32[32,128,256]{2,1,0:T(8,128)}, u32[]{:S(2)}, u32[]{:S(2)}) async-start(f32[32,128,256]{2,1,0:T(8,128)} %copy-done.7), calls=%async_computation.2 | async-start | bytes 8388608 | tf_op jit(solution)/shard_map/all_to_all | solution.py:245
  77.6 6.1 %shard_map.130 = (f32[2,128,256]{2,1,0:T(8,128)S(1)}, f32[2,128,256]{2,1,0:T(8,128)S(1)}, f32[2,128,256]{2,1,0:T(8,128)S(1)}, f32[2,128,256]{2,1,0:T(8,128)S(1)}) custom-call(s32[1]{0:T(128)} %bitcast.rank, s32[1]{0:T(128)} %bitcast.16.count, s32[128]{0:T(128)S(1)} %bitcast.37, s32[128]{0:T(128)S(1)} %bitcast.41, f32[8,128,256]{2,1,0:T(8,128)S(1)} %get-tuple-element.32.own, ...), custom_call_target="tpu_custom_call" | custom-call | bytes 50400000 | tf_op jit(solution)/shard_map/pallas_call | solution.py:223
  83.7 4.5 %collective-permute-start.2 = (f32[2,128,256]{2,1,0:T(8,128)S(1)}, f32[2,128,256]{2,1,0:T(8,128)S(1)}, u32[]{:S(2)}, u32[]{:S(2)}) collective-permute-start(f32[2,128,256]{2,1,0:T(8,128)S(1)} %get-tuple-element.37), channel_id=1, source_target_pairs={{0,3},{1,0},{2,1},{3,2},{4,7},{5,4},{6,5},{7,6},{8,11},{9,8},{10,9... | collective-permute-start | bytes 786440 | tf_op jit(solution)/shard_map/ppermute | solution.py:236
  88.2 3.9 %collective-permute-start.1 = (f32[2,128,256]{2,1,0:T(8,128)S(1)}, f32[2,128,256]{2,1,0:T(8,128)S(1)}, u32[]{:S(2)}, u32[]{:S(2)}) collective-permute-start(f32[2,128,256]{2,1,0:T(8,128)S(1)} %get-tuple-element.36), channel_id=1, source_target_pairs={{0,2},{1,3},{2,0},{3,1},{4,6},{5,7},{6,4},{7,5},{8,10},{9,11},{10,... | collective-permute-start | bytes 786440 | tf_op jit(solution)/shard_map/ppermute | solution.py:236
  93.4 6.8 %collective-permute-done.2 = f32[2,128,256]{2,1,0:T(8,128)S(1)} collective-permute-done((f32[2,128,256]{2,1,0:T(8,128)S(1)}, f32[2,128,256]{2,1,0:T(8,128)S(1)}, u32[]{:S(2)}, u32[]{:S(2)}) %collective-permute-start.2) | collective-permute-done | bytes 262176 | tf_op jit(solution)/shard_map/ppermute | solution.py:236
  100.2 4.1 %collective-permute-done = f32[2,128,256]{2,1,0:T(8,128)S(1)} collective-permute-done((f32[2,128,256]{2,1,0:T(8,128)S(1)}, f32[2,128,256]{2,1,0:T(8,128)S(1)}, u32[]{:S(2)}, u32[]{:S(2)}) %collective-permute-start) | collective-permute-done | bytes 262176 | tf_op jit(solution)/shard_map/ppermute | solution.py:236
  107.7 11.9 %collective-permute-done.3.q1 = f32[2,128,256]{2,1,0:T(8,128)S(1)} collective-permute-done((f32[2,128,256]{2,1,0:T(8,128)S(1)}, f32[2,128,256]{2,1,0:T(8,128)S(1)}, u32[]{:S(2)}, u32[]{:S(2)}) %collective-permute-start.3) | collective-permute-done | bytes 262176 | tf_op jit(solution)/shard_map/ppermute | solution.py:236
  124.4 4.4 %all-to-all-done.2.returned = f32[32,128,256]{2,1,0:T(8,128)} async-done(((f32[32,128,256]{2,1,0:T(8,128)}), f32[32,128,256]{2,1,0:T(8,128)}, u32[]{:S(2)}, u32[]{:S(2)}) %all-to-all-start.2) | async-done | bytes 4194336 | tf_op jit(solution)/shard_map/all_to_all | solution.py:245
  128.8 4.9 %all-to-all-start.1 = ((f32[32,128,256]{2,1,0:T(8,128)}), f32[32,128,256]{2,1,0:T(8,128)}, u32[]{:S(2)}, u32[]{:S(2)}) async-start(f32[32,128,256]{2,1,0:T(8,128)} %copy-done.8), calls=%async_computation.1 | async-start | bytes 8388608 | tf_op jit(solution)/shard_map/all_to_all | solution.py:245
  142.4 9.9 %collective-permute-done.14 = f32[2,128,256]{2,1,0:T(8,128)S(1)} collective-permute-done((f32[2,128,256]{2,1,0:T(8,128)S(1)}, f32[2,128,256]{2,1,0:T(8,128)S(1)}, u32[]{:S(2)}, u32[]{:S(2)}) %collective-permute-start.14) | collective-permute-done | bytes 262176 | tf_op jit(solution)/shard_map/ppermute | solution.py:236
  159.4 11.9 %collective-permute-done.15.q1 = f32[2,128,256]{2,1,0:T(8,128)S(1)} collective-permute-done((f32[2,128,256]{2,1,0:T(8,128)S(1)}, f32[2,128,256]{2,1,0:T(8,128)S(1)}, u32[]{:S(2)}, u32[]{:S(2)}) %collective-permute-start.15) | collective-permute-done | bytes 262176 | tf_op jit(solution)/shard_map/ppermute | solution.py:236
  175.3 5.4 %shard_map.136 = (f32[8,128,256]{2,1,0:T(8,128)S(1)}, f32[32,128,256]{2,1,0:T(8,128)S(1)}) custom-call(s32[1]{0:T(128)} %bitcast.rank, s32[1]{0:T(128)} %bitcast.19.count, s32[128]{0:T(128)S(1)} %bitcast.38, s32[128]{0:T(128)S(1)} %bitcast.42, f32[8,128,1]{2,1,0:T(8,128)S(1)} %copy.16.scale, f32[8,128,256]{2,1,0:T(8,128)S(1)} %bitcast.28, ...), custom_call_target="tpu_custom_call" | custom-call | bytes 50400000 | tf_op jit(solution)/shard_map/pallas_call | solution.py:223
  183.7 4.5 %all-to-all-done.1.arrived = f32[32,128,256]{2,1,0:T(8,128)} async-done(((f32[32,128,256]{2,1,0:T(8,128)}), f32[32,128,256]{2,1,0:T(8,128)}, u32[]{:S(2)}, u32[]{:S(2)}) %all-to-all-start.1) | async-done | bytes 4194336 | tf_op jit(solution)/shard_map/all_to_all | solution.py:245
  188.2 6.1 %all-to-all-start.3 = ((f32[32,128,256]{2,1,0:T(8,128)}), f32[32,128,256]{2,1,0:T(8,128)}, u32[]{:S(2)}, u32[]{:S(2)}) async-start(f32[32,128,256]{2,1,0:T(8,128)} %copy-done.9), calls=%async_computation.3 | async-start | bytes 8388608 | tf_op jit(solution)/shard_map/all_to_all | solution.py:245
  197.6 6.7 %shard_map.132 = (f32[2,128,256]{2,1,0:T(8,128)S(1)}, f32[2,128,256]{2,1,0:T(8,128)S(1)}, f32[2,128,256]{2,1,0:T(8,128)S(1)}, f32[2,128,256]{2,1,0:T(8,128)}) custom-call(s32[1]{0:T(128)} %bitcast.rank, s32[1]{0:T(128)} %bitcast.17.count, s32[128]{0:T(128)S(1)} %bitcast.39, s32[128]{0:T(128)S(1)} %bitcast.43, f32[8,128,256]{2,1,0:T(8,128)S(1)} %get-tuple-element.39.own, ...), custom_call_target="tpu_custom_call" | custom-call | bytes 50400000 | tf_op jit(solution)/shard_map/pallas_call | solution.py:223
  204.4 5.9 %collective-permute-start.8 = (f32[2,128,256]{2,1,0:T(8,128)}, f32[2,128,256]{2,1,0:T(8,128)}, u32[]{:S(2)}, u32[]{:S(2)}) collective-permute-start(f32[2,128,256]{2,1,0:T(8,128)} %get-tuple-element.44), channel_id=1, source_target_pairs={{0,3},{1,0},{2,1},{3,2},{4,7},{5,4},{6,5},{7,6},{8,11},{9,8},{10,9... | collective-permute-start | bytes 786440 | tf_op jit(solution)/shard_map/ppermute | solution.py:236
  214.2 34.6 %all-to-all-done.3.returned = f32[32,128,256]{2,1,0:T(8,128)} async-done(((f32[32,128,256]{2,1,0:T(8,128)}), f32[32,128,256]{2,1,0:T(8,128)}, u32[]{:S(2)}, u32[]{:S(2)}) %all-to-all-start.3) | async-done | bytes 4194336 | tf_op jit(solution)/shard_map/all_to_all | solution.py:245
  253.0 4.5 %collective-permute-start.20 = (f32[2,128,256]{2,1,0:T(8,128)S(1)}, f32[2,128,256]{2,1,0:T(8,128)S(1)}, u32[]{:S(2)}, u32[]{:S(2)}) collective-permute-start(f32[2,128,256]{2,1,0:T(8,128)S(1)} %get-tuple-element.56), channel_id=1, source_target_pairs={{0,3},{1,0},{2,1},{3,2},{4,7},{5,4},{6,5},{7,6},{8,11},{9,8},{10,9... | collective-permute-start | bytes 786440 | tf_op jit(solution)/shard_map/ppermute | solution.py:236
  263.5 10.6 %collective-permute-done.20 = f32[2,128,256]{2,1,0:T(8,128)S(1)} collective-permute-done((f32[2,128,256]{2,1,0:T(8,128)S(1)}, f32[2,128,256]{2,1,0:T(8,128)S(1)}, u32[]{:S(2)}, u32[]{:S(2)}) %collective-permute-start.20) | collective-permute-done | bytes 262176 | tf_op jit(solution)/shard_map/ppermute | solution.py:236
  281.2 3.9 %collective-permute-done.10.q2 = f32[2,128,256]{2,1,0:T(8,128)S(1)} collective-permute-done((f32[2,128,256]{2,1,0:T(8,128)S(1)}, f32[2,128,256]{2,1,0:T(8,128)S(1)}, u32[]{:S(2)}, u32[]{:S(2)}) %collective-permute-start.10) | collective-permute-done | bytes 262176 | tf_op jit(solution)/shard_map/ppermute | solution.py:236
  285.2 5.1 %collective-permute-done.11.q3 = f32[2,128,256]{2,1,0:T(8,128)S(1)} collective-permute-done((f32[2,128,256]{2,1,0:T(8,128)S(1)}, f32[2,128,256]{2,1,0:T(8,128)S(1)}, u32[]{:S(2)}, u32[]{:S(2)}) %collective-permute-start.11) | collective-permute-done | bytes 262176 | tf_op jit(solution)/shard_map/ppermute | solution.py:236
  (94 shorter events, 80.2 us)
Async XLA Ops:
  6.6 62.8 %all-to-all-start = ((f32[32,128,256]{2,1,0:T(8,128)}), f32[32,128,256]{2,1,0:T(8,128)}, u32[]{:S(2)}, u32[]{:S(2)}) async-start(f32[32,128,256]{2,1,0:T(8,128)} %copy-done.10), calls=%async_computation | async-start | bytes 8388608 | tf_op jit(solution)/shard_map/all_to_all | solution.py:245
  69.4 59.4 %all-to-all-start.2 = ((f32[32,128,256]{2,1,0:T(8,128)}), f32[32,128,256]{2,1,0:T(8,128)}, u32[]{:S(2)}, u32[]{:S(2)}) async-start(f32[32,128,256]{2,1,0:T(8,128)} %copy-done.7), calls=%async_computation.2 | async-start | bytes 8388608 | tf_op jit(solution)/shard_map/all_to_all | solution.py:245
  83.7 16.5 %collective-permute-start.2 = (f32[2,128,256]{2,1,0:T(8,128)S(1)}, f32[2,128,256]{2,1,0:T(8,128)S(1)}, u32[]{:S(2)}, u32[]{:S(2)}) collective-permute-start(f32[2,128,256]{2,1,0:T(8,128)S(1)} %get-tuple-element.37), channel_id=1, source_target_pairs={{0,3},{1,0},{2,1},{3,2},{4,7},{5,4},{6,5},{7,6},{8,11},{9,8},{10,9... | collective-permute-start | bytes 786440 | tf_op jit(solution)/shard_map/ppermute | solution.py:236
  104.4 15.2 %collective-permute-start.3 = (f32[2,128,256]{2,1,0:T(8,128)S(1)}, f32[2,128,256]{2,1,0:T(8,128)S(1)}, u32[]{:S(2)}, u32[]{:S(2)}) collective-permute-start(f32[2,128,256]{2,1,0:T(8,128)S(1)} %add_add_fusion.3.q0), channel_id=1, source_target_pairs={{0,1},{1,2},{2,3},{3,0},{4,5},{5,6},{6,7},{7,4},{8,9},{9,10},{10,1... | collective-permute-start | bytes 786440 | tf_op jit(solution)/shard_map/ppermute | solution.py:236
  104.5 15.2 %collective-permute-start.4 = (f32[2,128,256]{2,1,0:T(8,128)S(1)}, f32[2,128,256]{2,1,0:T(8,128)S(1)}, u32[]{:S(2)}, u32[]{:S(2)}) collective-permute-start(f32[2,128,256]{2,1,0:T(8,128)S(1)} %add_add_fusion.3.q0), channel_id=1, source_target_pairs={{0,2},{1,3},{2,0},{3,1},{4,6},{5,7},{6,4},{7,5},{8,10},{9,11},{10,... | collective-permute-start | bytes 786440 | tf_op jit(solution)/shard_map/ppermute | solution.py:236
  106.6 13.7 %collective-permute-start.5 = (f32[2,128,256]{2,1,0:T(8,128)S(1)}, f32[2,128,256]{2,1,0:T(8,128)S(1)}, u32[]{:S(2)}, u32[]{:S(2)}) collective-permute-start(f32[2,128,256]{2,1,0:T(8,128)S(1)} %add_add_fusion.3.q0), channel_id=1, source_target_pairs={{0,3},{1,0},{2,1},{3,2},{4,7},{5,4},{6,5},{7,6},{8,11},{9,8},{10,9... | collective-permute-start | bytes 786440 | tf_op jit(solution)/shard_map/ppermute | solution.py:236
  128.8 59.4 %all-to-all-start.1 = ((f32[32,128,256]{2,1,0:T(8,128)}), f32[32,128,256]{2,1,0:T(8,128)}, u32[]{:S(2)}, u32[]{:S(2)}) async-start(f32[32,128,256]{2,1,0:T(8,128)} %copy-done.8), calls=%async_computation.1 | async-start | bytes 8388608 | tf_op jit(solution)/shard_map/all_to_all | solution.py:245
  137.7 14.6 %collective-permute-start.14 = (f32[2,128,256]{2,1,0:T(8,128)S(1)}, f32[2,128,256]{2,1,0:T(8,128)S(1)}, u32[]{:S(2)}, u32[]{:S(2)}) collective-permute-start(f32[2,128,256]{2,1,0:T(8,128)S(1)} %get-tuple-element.50), channel_id=1, source_target_pairs={{0,3},{1,0},{2,1},{3,2},{4,7},{5,4},{6,5},{7,6},{8,11},{9,8},{10,9... | collective-permute-start | bytes 786440 | tf_op jit(solution)/shard_map/ppermute | solution.py:236
  141.5 14.6 %collective-permute-start.12 = (f32[2,128,256]{2,1,0:T(8,128)S(1)}, f32[2,128,256]{2,1,0:T(8,128)S(1)}, u32[]{:S(2)}, u32[]{:S(2)}) collective-permute-start(f32[2,128,256]{2,1,0:T(8,128)S(1)} %get-tuple-element.48), channel_id=1, source_target_pairs={{0,1},{1,2},{2,3},{3,0},{4,5},{5,6},{6,7},{7,4},{8,9},{9,10},{10,1... | collective-permute-start | bytes 786440 | tf_op jit(solution)/shard_map/ppermute | solution.py:236
  156.1 15.2 %collective-permute-start.15 = (f32[2,128,256]{2,1,0:T(8,128)S(1)}, f32[2,128,256]{2,1,0:T(8,128)S(1)}, u32[]{:S(2)}, u32[]{:S(2)}) collective-permute-start(f32[2,128,256]{2,1,0:T(8,128)S(1)} %add_add_fusion.1.q0), channel_id=1, source_target_pairs={{0,1},{1,2},{2,3},{3,0},{4,5},{5,6},{6,7},{7,4},{8,9},{9,10},{10,1... | collective-permute-start | bytes 786440 | tf_op jit(solution)/shard_map/ppermute | solution.py:236
  156.2 15.2 %collective-permute-start.16 = (f32[2,128,256]{2,1,0:T(8,128)S(1)}, f32[2,128,256]{2,1,0:T(8,128)S(1)}, u32[]{:S(2)}, u32[]{:S(2)}) collective-permute-start(f32[2,128,256]{2,1,0:T(8,128)S(1)} %add_add_fusion.1.q0), channel_id=1, source_target_pairs={{0,2},{1,3},{2,0},{3,1},{4,6},{5,7},{6,4},{7,5},{8,10},{9,11},{10,... | collective-permute-start | bytes 786440 | tf_op jit(solution)/shard_map/ppermute | solution.py:236
  158.2 13.7 %collective-permute-start.17 = (f32[2,128,256]{2,1,0:T(8,128)S(1)}, f32[2,128,256]{2,1,0:T(8,128)S(1)}, u32[]{:S(2)}, u32[]{:S(2)}) collective-permute-start(f32[2,128,256]{2,1,0:T(8,128)S(1)} %add_add_fusion.1.q0), channel_id=1, source_target_pairs={{0,3},{1,0},{2,1},{3,2},{4,7},{5,4},{6,5},{7,6},{8,11},{9,8},{10,9... | collective-permute-start | bytes 786440 | tf_op jit(solution)/shard_map/ppermute | solution.py:236
  188.2 60.6 %all-to-all-start.3 = ((f32[32,128,256]{2,1,0:T(8,128)}), f32[32,128,256]{2,1,0:T(8,128)}, u32[]{:S(2)}, u32[]{:S(2)}) async-start(f32[32,128,256]{2,1,0:T(8,128)} %copy-done.9), calls=%async_computation.3 | async-start | bytes 8388608 | tf_op jit(solution)/shard_map/all_to_all | solution.py:245
  204.4 53.2 %collective-permute-start.8 = (f32[2,128,256]{2,1,0:T(8,128)}, f32[2,128,256]{2,1,0:T(8,128)}, u32[]{:S(2)}, u32[]{:S(2)}) collective-permute-start(f32[2,128,256]{2,1,0:T(8,128)} %get-tuple-element.44), channel_id=1, source_target_pairs={{0,3},{1,0},{2,1},{3,2},{4,7},{5,4},{6,5},{7,6},{8,11},{9,8},{10,9... | collective-permute-start | bytes 786440 | tf_op jit(solution)/shard_map/ppermute | solution.py:236
  210.3 48.4 %collective-permute-start.7 = (f32[2,128,256]{2,1,0:T(8,128)S(1)}, f32[2,128,256]{2,1,0:T(8,128)}, u32[]{:S(2)}, u32[]{:S(2)}) collective-permute-start(f32[2,128,256]{2,1,0:T(8,128)S(1)} %get-tuple-element.43), channel_id=1, source_target_pairs={{0,2},{1,3},{2,0},{3,1},{4,6},{5,7},{6,4},{7,5},{8,10},{9,11},{10,... | collective-permute-start | bytes 786440 | tf_op jit(solution)/shard_map/ppermute | solution.py:236
  212.9 45.8 %collective-permute-start.6 = (f32[2,128,256]{2,1,0:T(8,128)S(1)}, f32[2,128,256]{2,1,0:T(8,128)}, u32[]{:S(2)}, u32[]{:S(2)}) collective-permute-start(f32[2,128,256]{2,1,0:T(8,128)S(1)} %get-tuple-element.42), channel_id=1, source_target_pairs={{0,1},{1,2},{2,3},{3,0},{4,5},{5,6},{6,7},{7,4},{8,9},{9,10},{10,1... | collective-permute-start | bytes 786440 | tf_op jit(solution)/shard_map/ppermute | solution.py:236
  253.0 21.1 %collective-permute-start.20 = (f32[2,128,256]{2,1,0:T(8,128)S(1)}, f32[2,128,256]{2,1,0:T(8,128)S(1)}, u32[]{:S(2)}, u32[]{:S(2)}) collective-permute-start(f32[2,128,256]{2,1,0:T(8,128)S(1)} %get-tuple-element.56), channel_id=1, source_target_pairs={{0,3},{1,0},{2,1},{3,2},{4,7},{5,4},{6,5},{7,6},{8,11},{9,8},{10,9... | collective-permute-start | bytes 786440 | tf_op jit(solution)/shard_map/ppermute | solution.py:236
  257.6 20.3 %collective-permute-start.19 = (f32[2,128,256]{2,1,0:T(8,128)S(1)}, f32[2,128,256]{2,1,0:T(8,128)S(1)}, u32[]{:S(2)}, u32[]{:S(2)}) collective-permute-start(f32[2,128,256]{2,1,0:T(8,128)S(1)} %get-tuple-element.55), channel_id=1, source_target_pairs={{0,2},{1,3},{2,0},{3,1},{4,6},{5,7},{6,4},{7,5},{8,10},{9,11},{10,... | collective-permute-start | bytes 786440 | tf_op jit(solution)/shard_map/ppermute | solution.py:236
  257.6 20.3 %collective-permute-start.18 = (f32[2,128,256]{2,1,0:T(8,128)S(1)}, f32[2,128,256]{2,1,0:T(8,128)S(1)}, u32[]{:S(2)}, u32[]{:S(2)}) collective-permute-start(f32[2,128,256]{2,1,0:T(8,128)S(1)} %get-tuple-element.54), channel_id=1, source_target_pairs={{0,1},{1,2},{2,3},{3,0},{4,5},{5,6},{6,7},{7,4},{8,9},{9,10},{10,1... | collective-permute-start | bytes 786440 | tf_op jit(solution)/shard_map/ppermute | solution.py:236
  259.9 19.6 %collective-permute-start.9 = (f32[2,128,256]{2,1,0:T(8,128)S(1)}, f32[2,128,256]{2,1,0:T(8,128)S(1)}, u32[]{:S(2)}, u32[]{:S(2)}) collective-permute-start(f32[2,128,256]{2,1,0:T(8,128)S(1)} %add_add_fusion.2.q0), channel_id=1, source_target_pairs={{0,1},{1,2},{2,3},{3,0},{4,5},{5,6},{6,7},{7,4},{8,9},{9,10},{10,1... | collective-permute-start | bytes 786440 | tf_op jit(solution)/shard_map/ppermute | solution.py:236
  262.3 22.9 %collective-permute-start.10 = (f32[2,128,256]{2,1,0:T(8,128)S(1)}, f32[2,128,256]{2,1,0:T(8,128)S(1)}, u32[]{:S(2)}, u32[]{:S(2)}) collective-permute-start(f32[2,128,256]{2,1,0:T(8,128)S(1)} %add_add_fusion.2.q0), channel_id=1, source_target_pairs={{0,2},{1,3},{2,0},{3,1},{4,6},{5,7},{6,4},{7,5},{8,10},{9,11},{10,... | collective-permute-start | bytes 786440 | tf_op jit(solution)/shard_map/ppermute | solution.py:236
  274.2 16.1 %collective-permute-start.11 = (f32[2,128,256]{2,1,0:T(8,128)S(1)}, f32[2,128,256]{2,1,0:T(8,128)S(1)}, u32[]{:S(2)}, u32[]{:S(2)}) collective-permute-start(f32[2,128,256]{2,1,0:T(8,128)S(1)} %add_add_fusion.2.q0), channel_id=1, source_target_pairs={{0,3},{1,0},{2,1},{3,2},{4,7},{5,4},{6,5},{7,6},{8,11},{9,8},{10,9... | collective-permute-start | bytes 786440 | tf_op jit(solution)/shard_map/ppermute | solution.py:236
  278.0 16.8 %collective-permute-start.22 = (f32[2,128,256]{2,1,0:T(8,128)S(1)}, f32[2,128,256]{2,1,0:T(8,128)S(1)}, u32[]{:S(2)}, u32[]{:S(2)}) collective-permute-start(f32[2,128,256]{2,1,0:T(8,128)S(1)} %add_add_fusion.q0), channel_id=1, source_target_pairs={{0,2},{1,3},{2,0},{3,1},{4,6},{5,7},{6,4},{7,5},{8,10},{9,11},{10,... | collective-permute-start | bytes 786440 | tf_op jit(solution)/shard_map/ppermute | solution.py:236
  279.5 15.3 %collective-permute-start.23 = (f32[2,128,256]{2,1,0:T(8,128)S(1)}, f32[2,128,256]{2,1,0:T(8,128)S(1)}, u32[]{:S(2)}, u32[]{:S(2)}) collective-permute-start(f32[2,128,256]{2,1,0:T(8,128)S(1)} %add_add_fusion.q0), channel_id=1, source_target_pairs={{0,3},{1,0},{2,1},{3,2},{4,7},{5,4},{6,5},{7,6},{8,11},{9,8},{10,9... | collective-permute-start | bytes 786440 | tf_op jit(solution)/shard_map/ppermute | solution.py:236
  (27 other events, 358.5 us)
